TPU v7x, 32 devices: a whole 2x2x4 slice. The times are simulated.
32 devices in a mesh: group: 1, expert: 16 (over z, y, x), dp: 2 (over core).
Axes of the slice: x: 2, y: 2, z: 4, core: 2. Of those that a mesh axis runs over, the one named last changes fastest.
Arguments:
- tokens: bfloat16 [4, 256, 4096], P(None, ('group', 'expert', 'dp')), may hold values from -6 to 6
- routes: int32 [4, 256, 8], P(None, ('group', 'expert', 'dp')), may hold values from 0 to 15, all different within a row; in each aligned block of 8 rows (0 to 7, 8 to 15, ..., all dimensions but the last counted through in order) at most 4 rows name the same one
- route_weights: float32 [4, 256, 8], P(None, ('group', 'expert', 'dp')), may hold values from 0.05 to 1
- live_rows: int32 [4, 32], P(None, ('group', 'expert', 'dp')), may hold values from 4 to 8, as said below
- gate_weight: bfloat16 [16, 4096, 768], P('expert', None, 'dp'), may hold values from -0.09375 to 0.09375
- up_weight: bfloat16 [16, 4096, 768], P('expert', None, 'dp'), may hold values from -0.09375 to 0.09375
- down_weight: bfloat16 [16, 768, 4096], P('expert', 'dp'), may hold values from -0.21875 to 0.21875
Outputs:
- mixed: bfloat16 [4, 256, 4096], P(None, ('group', 'expert', 'dp'))
Inputs may be any that keep to these rules, and one draw needn't show every extreme that they name: `routes`: in each step, of the 8 rows of one device at most 4 name any one expert, a bound that some block reaches of them; a row names 8 different experts. `live_rows`: in each step some device has all 8 rows live.
All inputs are finite; a program needn't handle non-finite values.
Results may differ from a plain program's by a relative error of at most 0.0059.
Values may be sent and summed in bfloat16 or wider, within the bound.
A program may use at most 128 MiB of HBM per device.

v0:
```python
import jax
import jax.numpy as jnp
from jax import lax
from jax.sharding import PartitionSpec as P


def owner_scales(routes, route_weights, live_rows, experts_count):
    row_count = routes.shape[1]
    norm = route_weights / jnp.sum(route_weights, axis=-1, keepdims=True)
    alive = jnp.arange(row_count, dtype=jnp.int32)[None, :] < live_rows
    hit = routes[..., None] == jnp.arange(experts_count, dtype=jnp.int32)
    hit = hit & alive[:, :, None, None]
    return jnp.sum(jnp.where(hit, norm[..., None], 0.0), axis=2)


def shards(tokens, routes, route_weights, live_rows, gate_weight, up_weight, down_weight):
    steps, row_count, width = tokens.shape
    experts_count = lax.axis_size("expert")
    me = lax.axis_index("expert")
    gate_w, up_w, down_w = gate_weight[0], up_weight[0], down_weight[0]
    scales = owner_scales(routes, route_weights, live_rows, experts_count)
    all_scales = lax.all_gather(scales, ("expert", "dp"), axis=1, tiled=True)
    mine = jnp.sum(
        jnp.where(jnp.arange(experts_count) == me, all_scales, 0.0), axis=-1
    )
    rows = lax.all_gather(tokens, ("expert", "dp"), axis=1, tiled=True)
    rows_all = rows.shape[1]
    flat = rows.reshape(steps * rows_all, width)
    gate = jnp.dot(flat, gate_w, preferred_element_type=jnp.float32)
    up = jnp.dot(flat, up_w, preferred_element_type=jnp.float32)
    hidden = (jax.nn.silu(gate) * up).astype(jnp.bfloat16)
    part = jnp.dot(hidden, down_w, preferred_element_type=jnp.float32)
    part = part * mine.reshape(steps * rows_all, 1)
    part = part.reshape(steps, rows_all, width).astype(jnp.bfloat16)
    return lax.psum_scatter(part, ("expert", "dp"), scatter_dimension=1, tiled=True)


def solution(mesh):
    spread = ("group", "expert", "dp")
    in_specs = (
        P(None, spread, None),
        P(None, spread, None),
        P(None, spread, None),
        P(None, spread),
        P("expert", None, "dp"),
        P("expert", None, "dp"),
        P("expert", "dp", None),
    )
    out_specs = P(None, spread, None)
    return jax.shard_map(shards, mesh=mesh, in_specs=in_specs, out_specs=out_specs, check_vma=False)
```

profile of v0, /device:TPU:0, one launch (start us, length us, event | category | flops | bytes accessed | tf_op | source)
XLA Modules:
  0.0 299.4 jit_solution(17416889410807359160)
XLA Ops:
  6.5 0.0 copy-start
  6.5 0.0 all-gather.2.cloned.1.call-start
  6.5 0.7 all-gather.2.cloned.1.call-update
  7.3 0.0 reduce-scatter.4.cloned.1.call-start
  7.3 0.9 iota_compare_fusion.1
  8.2 0.9 fusion.9
  9.1 0.9 select_reduce_fusion.1
  10.0 45.5 %all_gather.7 = f32[4,256,16]{2,1,0:T(8,128)S(1)} all-gather(f32[4,8,16]{2,1,0:T(8,128)S(1)} %select_reduce_fusion.1), channel_id=1, replica_groups=mesh['group'=1,'expert'=16,'dp'=2] {'expert','dp'}, dimensions={1}, use_global_device_ids=true | all-gather | bytes 67584 | tf_op jit(solution)/shard_map/all_gather | solution.py:22
  55.5 0.2 select_reduce_fusion
  55.7 35.7 %all-gather.2.cloned.1.call-done = bf16[4,256,4096]{2,1,0:T(8,128)(2,1)} async-done(((bf16[4,8,4096]{2,1,0:T(8,128)(2,1)}), bf16[4,256,4096]{2,1,0:T(8,128)(2,1)}) %all-gather.2.cloned.1.call-update) | async-done | bytes 8388624 | tf_op jit(solution)/shard_map/all_gather | solution.py:26
  91.4 0.0 copy-start.1
  91.4 0.0 copy-start.2
  91.4 8.0 %fusion.3 = f32[1024,384]{1,0:T(8,128)S(1)} fusion(bf16[1024,4096]{1,0:T(8,128)(2,1)} %bitcast.30, bf16[1,4096,384]{2,1,0:T(8,128)(2,1)} %param.11), kind=kOutput, calls=%fused_computation.4 | convolution fusion | flops 3221225472 | bytes 13107200 | tf_op jit(solution)/shard_map/dot_general | solution.py:29
  99.4 0.0 copy-done.1
  99.4 0.0 copy-done.2
  99.4 4.6 %multiply_convert_fusion.1 = bf16[1024,384]{1,0:T(8,128)(2,1)S(1)} fusion(f32[1024,384]{1,0:T(8,128)S(1)} %fusion.3, bf16[1024,4096]{1,0:T(8,128)(2,1)S(1)} %bitcast.31, bf16[1,4096,384]{2,1,0:T(8,128)(2,1)S(1)} %copy-done.2), kind=kOutput, calls=%fused_computation.6 | convolution fusion | flops 3223584768 | bytes 13893632 | tf_op jit(solution)/shard_map/dot_general | solution.py:30
  104.0 0.0 copy-done
  104.0 4.7 %multiply_convert_fusion = bf16[1024,4096]{1,0:T(8,128)(2,1)S(1)} fusion(bf16[1024,384]{1,0:T(8,128)(2,1)S(1)} %multiply_convert_fusion.1, f32[1024]{0:T(1024)S(1)} %bitcast.29, bf16[1,384,4096]{2,1,0:T(8,128)(2,1)S(1)} %copy-done), kind=kOutput, calls=%fused_computation | convolution fusion | flops 3229614080 | bytes 12324864 | tf_op jit(solution)/shard_map/dot_general | solution.py:32
  108.7 19.1 %copy.9 = bf16[4,256,4096]{2,0,1:T(4,128)(2,1)} copy(bf16[4,256,4096]{2,1,0:T(8,128)(2,1)S(1)} %bitcast.26) | data formatting | bytes 16777216
  127.8 15.5 %copy.13 = bf16[32,8,4,4096]{3,1,2,0:T(8,128)(2,1)} copy(bf16[32,8,4,4096]{3,2,1,0:T(4,128)(2,1)} %bitcast.25) | data formatting | bytes 16777216
  143.2 0.0 reduce-scatter.4.cloned.1.call-update
  143.3 147.3 %reduce-scatter.4.cloned.1.call-done = bf16[8,16384]{1,0:T(8,128)(2,1)} async-done(((bf16[256,16384]{1,0:T(8,128)(2,1)}), bf16[8,16384]{1,0:T(8,128)(2,1)}) %reduce-scatter.4.cloned.1.call-update) | async-done | bytes 262160
  290.6 1.1 reshape.34
  291.7 0.9 copy.10
  (2 shorter events, 0.0 us)
Async XLA Ops:
  6.5 97.4 %copy-start = (bf16[1,384,4096]{2,1,0:T(8,128)(2,1)S(1)}, bf16[1,384,4096]{2,1,0:T(8,128)(2,1)}, u32[]{:S(2)}) copy-start(bf16[1,384,4096]{2,1,0:T(8,128)(2,1)} %param.13) | copy-start | bytes 9437188
  6.5 84.8 %all-gather.2.cloned.1.call-start = ((), (), s32[]{:S(2)}) async-start(), calls=%async_computation.1 | async-start | bytes 8650752 | tf_op jit(solution)/shard_map/all_gather | solution.py:26
  7.3 283.4 %reduce-scatter.4.cloned.1.call-start = ((), (), s32[]{:S(2)}) async-start(), calls=%async_computation.2 | async-start | bytes 8650752
  91.4 8.0 %copy-start.1 = (bf16[4,256,4096]{2,1,0:T(8,128)(2,1)S(1)}, bf16[4,256,4096]{2,1,0:T(8,128)(2,1)}, u32[]{:S(2)}) copy-start(bf16[4,256,4096]{2,1,0:T(8,128)(2,1)} %all-gather.2.cloned.1.call-done) | copy-start | bytes 25165828
  91.4 8.0 %copy-start.2 = (bf16[1,4096,384]{2,1,0:T(8,128)(2,1)S(1)}, bf16[1,4096,384]{2,1,0:T(8,128)(2,1)}, u32[]{:S(2)}) copy-start(bf16[1,4096,384]{2,1,0:T(8,128)(2,1)} %param.12) | copy-start | bytes 9437188
Sparse Core Ops, SparseCore 0:
  10.3 81.0 all-gather.1
  143.4 147.1 reduce-scatter.3
where the time goes:
time: 300 us; the launch traced here: 299 us
  waiting for transfers between devices  184 us (61%)
  blocking collectives  45.5 us (15%)
  local copies, waits for them, and re-layouts  36.6 us (12%)
  matrix products  17.3 us (6%)
  between operations  13.5 us (4%)
    unnamed x3, waiting for transfers between devices  148 us
    all_gather x1, blocking collectives, shards(): all_scales = lax.all_gather(scales, ('expert', 'dp'), axis=1, tiled=True)  45.5 us
    unnamed x11, local copies, waits for them, and re-layouts  36.6 us
    all_gather x1, waiting for transfers between devices, shards(): rows = lax.all_gather(tokens, ('expert', 'dp'), axis=1, tiled=True)  35.7 us
    dot_general x1, matrix products, shards(): gate = jnp.dot(flat, gate_w, preferred_element_type=jnp.float32)  7.97 us
  transfers between devices with their start and end apart: 2, of which 2 were waited for; matrix products, arithmetic and copies ran while one was open for 1% of the time, Pallas kernels for 0%

commit v1 on v0

--- a/solution.py
+++ b/solution.py
@@ -1,6 +1,10 @@
+import functools
+
 import jax
 import jax.numpy as jnp
 from jax import lax
+from jax.experimental import pallas as pl
+from jax.experimental.pallas import tpu as pltpu
 from jax.sharding import PartitionSpec as P
 
 
@@ -12,10 +16,237 @@
     hit = hit & alive[:, :, None, None]
     return jnp.sum(jnp.where(hit, norm[..., None], 0.0), axis=2)
 
+MESH = pl.DeviceIdType.MESH
+CHUNKS = 8
+TILE = 256
+VMEM_BYTES = 56 * 2**20
+
+
+def kernel(bits, chunks, tok, sc, gate_in, up_in, down_in, out,
+           got, part, landed, scales, wgu, wd, acc, hidden, scale_col,
+           ag_send, ag_recv, sc_send, sc_recv, rs_send, rs_recv,
+           w_send, w_recv, w_local, t_local):
+    me = lax.axis_index("expert")
+    core = lax.axis_index("dp")
+    other = {"dp": 1 - core}
+    bit = [(me // 2**b) % 2 for b in range(bits)]
+    partner = [{"expert": me + (1 - 2 * bit[b]) * 2**b} for b in range(bits)]
+    rows, width = tok.shape
+    cols = width // chunks
+    half = gate_in.shape[1]
+    full = 2 * half
+    total = 2**bits * rows
+
+    def gather_order(c):
+        low = [0, 1] if c % 2 == 0 else [1, 0]
+        return list(range(2, bits)) + low
+
+    def reduce_order(c):
+        return gather_order(c)[::-1]
+
+    def place(free, flip=None):
+        index = []
+        for b in range(bits - 1, -1, -1):
+            if b in free:
+                index.append(slice(None))
+            elif b == flip:
+                index.append(1 - bit[b])
+            else:
+                index.append(bit[b])
+        return tuple(index)
+
+    barrier = pltpu.get_barrier_semaphore()
+    for b in range(bits):
+        pl.semaphore_signal(barrier, inc=1, device_id=partner[b], device_id_type=MESH)
+    pl.semaphore_signal(barrier, inc=1, device_id=other, device_id_type=MESH)
+
+    own = place(())
+    locals_ = [pltpu.make_async_copy(tok.at[:, pl.ds(c * cols, cols)], got.at[(c, *own)], t_local.at[c])
+               for c in range(chunks)]
+    locals_.append(pltpu.make_async_copy(sc, scales.at[own], t_local.at[chunks]))
+    for copy in locals_:
+        copy.start()
+    sources = [gate_in, up_in, down_in]
+
+    def weight_slot(i, which):
+        if i < 2:
+            return wgu.at[:, pl.ds(i * full + which * half, half)]
+        return wd.at[pl.ds(which * half, half), :]
+
+    w_own = [pltpu.make_async_copy(sources[i], weight_slot(i, 0), w_local.at[i]) for i in range(3)]
+    for copy in w_own:
+        copy.start()
+    pl.semaphore_wait(barrier, bits + 1)
+
+    def ag_copy(c, level):
+        order = gather_order(c)
+        index = (c, *place(order[:level]))
+        return pltpu.make_async_remote_copy(
+            src_ref=got.at[index], dst_ref=got.at[index],
+            send_sem=ag_send.at[c, level], recv_sem=ag_recv.at[c, level],
+            device_id=partner[order[level]], device_id_type=MESH)
+
+    def sc_copy(level):
+        order = gather_order(0)
+        index = place(order[:level])
+        return pltpu.make_async_remote_copy(
+            src_ref=scales.at[index], dst_ref=scales.at[index],
+            send_sem=sc_send.at[level], recv_sem=sc_recv.at[level],
+            device_id=partner[order[level]], device_id_type=MESH)
+
+    def rs_copy(c, level):
+        order = reduce_order(c)
+        rest = order[level + 1:]
+        b = order[level]
+        return pltpu.make_async_remote_copy(
+            src_ref=part.at[(c, *place(rest, b))], dst_ref=landed.at[(c, *place(rest))],
+            send_sem=rs_send.at[c, level], recv_sem=rs_recv.at[c, level],
+            device_id=partner[b], device_id_type=MESH)
+
+    for c in range(chunks):
+        locals_[c].wait()
+        ag_copy(c, 0).start()
+    locals_[chunks].wait()
+    sc_copy(0).start()
+    w_far = [pltpu.make_async_remote_copy(
+        src_ref=sources[i], dst_ref=weight_slot(i, 1), send_sem=w_send.at[i],
+        recv_sem=w_recv.at[i], device_id=other, device_id_type=MESH) for i in range(3)]
+    for copy in w_far:
+        copy.start()
+
+    for level in range(bits):
+        for c in range(chunks):
+            ag_copy(c, level).wait_recv()
+            if level + 1 < bits:
+                ag_copy(c, level + 1).start()
+                continue
+            if c == 0:
+                for i in range(2):
+                    w_own[i].wait()
+                    w_far[i].wait_recv()
+            def up_tile(j, _, c=c):
+                at = pl.ds(pl.multiple_of(j * TILE, TILE), TILE)
+                x = got[c].reshape(total, cols)
+                y = jnp.dot(x, wgu[pl.ds(c * cols, cols), at], preferred_element_type=jnp.float32)
+                if c == 0:
+                    acc[:, at] = y
+                else:
+                    acc[:, at] += y
+                return 0
+
+            lax.fori_loop(0, 2 * full // TILE, up_tile, 0)
+        sc_copy(level).wait_recv()
+        if level + 1 < bits:
+            sc_copy(level + 1).start()
+
+    def act_tile(j, _):
+        at = pl.ds(pl.multiple_of(j * 128, 128), 128)
+        gate = acc[:, at]
+        up = acc[:, pl.ds(pl.multiple_of(full + j * 128, 128), 128)]
+        hidden[:, at] = (gate / (1.0 + jnp.exp(-gate)) * up).astype(jnp.bfloat16)
+        return 0
+
+    lax.fori_loop(0, full // 128, act_tile, 0)
+    every = scales[...].reshape(total, scales.shape[-1])
+    lane = lax.broadcasted_iota(jnp.int32, every.shape, 1)
+    column = jnp.sum(jnp.where(lane == me, every, 0.0), axis=1, keepdims=True)
+    scale_col[...] = jnp.broadcast_to(column, scale_col.shape)
+    w_own[2].wait()
+    w_far[2].wait_recv()
+
+    for c in range(chunks):
+        def down_tile(j, _, c=c):
+            at = pl.ds(pl.multiple_of(c * cols + j * TILE, TILE), TILE)
+            y = jnp.dot(hidden[...], wd[:, at], preferred_element_type=jnp.float32)
+            y = (y * scale_col[:, :1]).astype(jnp.bfloat16)
+            to = (c, *([slice(None)] * (bits + 1)), pl.ds(pl.multiple_of(j * TILE, TILE), TILE))
+            part[to] = y.reshape((2,) * bits + (rows, TILE))
+            return 0
+
+        lax.fori_loop(0, cols // TILE, down_tile, 0)
+        rs_copy(c, 0).start()
+
+    for level in range(bits):
+        for c in range(chunks):
+            rs_copy(c, level).wait_recv()
+            order = reduce_order(c)
+            rest, b = order[level + 1:], order[level]
+            keep, came = (c, *place(rest)), (c, *place(rest, b))
+            value = part[keep].astype(jnp.float32) + landed[came].astype(jnp.float32)
+            if level + 1 < bits:
+                part[keep] = value.astype(jnp.bfloat16)
+                rs_copy(c, level + 1).start()
+            else:
+                out[:, pl.ds(c * cols, cols)] = value.astype(jnp.bfloat16)
+
+    for level in range(bits):
+        for c in range(chunks):
+            ag_copy(c, level).wait_send()
+            rs_copy(c, level).wait_send()
+        sc_copy(level).wait_send()
+    for copy in w_far:
+        copy.wait_send()
+
+
+def kernel_bytes(experts, rows, width, half):
+    block = experts * rows
+    return (3 * block * width * 2 + 3 * width * 2 * half * 2 + block * 4 * half * 4
+            + block * 2 * half * 2 + 2 * block * 128 * 4 + 2 * rows * width * 2)
+
+
+def fits(experts, rows, width, half, cores):
+    even = experts >= 4 and experts & (experts - 1) == 0 and experts <= 128 and cores == 2
+    return (even and rows % 16 == 0 and width % (CHUNKS * TILE) == 0 and half % 128 == 0
+            and kernel_bytes(experts, rows, width, half) < VMEM_BYTES - 8 * 2**20)
+
+
+def fused(tokens, routes, route_weights, live_rows, gate_weight, up_weight, down_weight):
+    steps, row_count, width = tokens.shape
+    experts = lax.axis_size("expert")
+    bits = experts.bit_length() - 1
+    rows = steps * row_count
+    half = gate_weight.shape[2]
+    scales = owner_scales(routes, route_weights, live_rows, experts)
+    scales = jnp.pad(scales.reshape(rows, experts), ((0, 0), (0, 128 - experts)))
+    cols = width // CHUNKS
+    total = experts * rows
+    grid = (2,) * bits
+    dma = pltpu.SemaphoreType.DMA
+    out = pl.pallas_call(
+        functools.partial(kernel, bits, CHUNKS),
+        out_shape=jax.ShapeDtypeStruct((rows, width), jnp.bfloat16),
+        in_specs=[pl.BlockSpec(memory_space=pltpu.VMEM)] * 2
+        + [pl.BlockSpec(memory_space=pl.ANY)] * 3,
+        out_specs=pl.BlockSpec(memory_space=pltpu.VMEM),
+        scratch_shapes=[
+            pltpu.VMEM((CHUNKS, *grid, rows, cols), jnp.bfloat16),
+            pltpu.VMEM((CHUNKS, *grid, rows, cols), jnp.bfloat16),
+            pltpu.VMEM((CHUNKS, *grid, rows, cols), jnp.bfloat16),
+            pltpu.VMEM((*grid, rows, 128), jnp.float32),
+            pltpu.VMEM((width, 4 * half), jnp.bfloat16),
+            pltpu.VMEM((2 * half, width), jnp.bfloat16),
+            pltpu.VMEM((total, 4 * half), jnp.float32),
+            pltpu.VMEM((total, 2 * half), jnp.bfloat16),
+            pltpu.VMEM((total, 128), jnp.float32),
+            dma((CHUNKS, bits)), dma((CHUNKS, bits)), dma((bits,)), dma((bits,)),
+            dma((CHUNKS, bits)), dma((CHUNKS, bits)), dma((3,)), dma((3,)), dma((3,)),
+            dma((CHUNKS + 1,)),
+        ],
+        compiler_params=pltpu.CompilerParams(
+            collective_id=0, has_side_effects=True, vmem_limit_bytes=VMEM_BYTES),
+        cost_estimate=pl.CostEstimate(
+            flops=12 * total * half * width, bytes_accessed=12 * half * width, transcendentals=0),
+    )(tokens.reshape(rows, width), scales, gate_weight[0], up_weight[0], down_weight[0])
+    return out.reshape(steps, row_count, width)
+
 
 def shards(tokens, routes, route_weights, live_rows, gate_weight, up_weight, down_weight):
     steps, row_count, width = tokens.shape
     experts_count = lax.axis_size("expert")
+    if fits(experts_count, steps * row_count, width, gate_weight.shape[2], lax.axis_size("dp")):
+        return fused(
+            tokens, routes, route_weights, live_rows, gate_weight, up_weight, down_weight
+        )
     me = lax.axis_index("expert")
     gate_w, up_w, down_w = gate_weight[0], up_weight[0], down_weight[0]
     scales = owner_scales(routes, route_weights, live_rows, experts_count)

time: 300 us -> 118 us (0.39)
  waiting for transfers between devices: 184 us -> 0 us
  Pallas kernels: 0 us -> 112 us
  blocking collectives: 45.5 us -> 0 us
  local copies, waits for them, and re-layouts: 36.6 us -> 2.28 us
  matrix products: 17.3 us -> 0 us
  between operations: 13.5 us -> 0.02 us
    unnamed x3 -> x0, waiting for transfers between devices: 148 us -> none
    pallas_call x0 -> x1, Pallas kernels: none -> 112 us  [fused(): pl.pallas_call(functools.partial(kernel, bits, CHUNKS), out_shape=jax.Sha...]
    all_gather x1 -> x0, blocking collectives: 45.5 us -> none  [shards(): all_scales = lax.all_gather(scales, ('expert', 'dp'), axis=1, tiled=True)]
    all_gather x1 -> x0, waiting for transfers between devices: 35.7 us -> none  [shards(): rows = lax.all_gather(tokens, ('expert', 'dp'), axis=1, tiled=True)]
    unnamed x11 -> x1, local copies, waits for them, and re-layouts: 36.6 us -> 1.67 us
    dot_general x3 -> x0, matrix products: 17.3 us -> none  [the longest x1 7.97 us: shards(): gate = jnp.dot(flat, gate_w, preferred_element_type=jnp.float32)]
  transfers between devices with their start and end apart: 2 -> 0, of which waited for: 2 -> 0; matrix products, arithmetic and copies ran while one was open for 1% -> 0% of each run, Pallas kernels for 0% -> 0%
where the time goes in v1:
time: 118 us; the launch traced here: 117 us
  Pallas kernels  112 us (95%)
  other arithmetic  2.5 us (2%)
  local copies, waits for them, and re-layouts  2.28 us (2%)
    pallas_call x1, Pallas kernels, fused(): pl.pallas_call(functools.partial(kernel, bits, CHUNKS), out_shape=jax.Sha...  112 us

profile of v1, /device:TPU:0, one launch (start us, length us, event | category | flops | bytes accessed | tf_op | source)
XLA Modules:
  0.0 117.1 jit_solution(866320626225949055)
XLA Ops:
  0.0 0.7 iota_compare_fusion.1
  0.7 0.9 fusion.2
  1.6 0.9 select_reduce_fusion
  2.5 0.6 pad.4.sc
  3.1 112.3 %shard_map.76 = bf16[32,4096]{1,0:T(8,128)(2,1)} custom-call(bf16[32,4096]{1,0:T(8,128)(2,1)} %bitcast.13, f32[32,128]{1,0:T(8,128)} %pad.4.sc, bf16[4096,384]{1,0:T(8,128)(2,1)} %bitcast.10, bf16[4096,384]{1,0:T(8,128)(2,1)} %bitcast.11, bf16[384,4096]{1,0:T(8,128)(2,1)} %bitcast.12), custom_call_target="tpu_custom_call" | custom-call | flops 9663676416 | bytes 18874368 | tf_op jit(solution)/shard_map/pallas_call | solution.py:215
  115.4 1.7 %copy.9 = bf16[4,8,4096]{2,1,0:T(8,128)(2,1)} copy(bf16[4,8,4096]{2,1,0:T(8,128)(2,1)} %bitcast.8) | data formatting | bytes 524288

commit v2 on v1

--- a/solution.py
+++ b/solution.py
@@ -17,8 +17,11 @@
     return jnp.sum(jnp.where(hit, norm[..., None], 0.0), axis=2)
 
 MESH = pl.DeviceIdType.MESH
-CHUNKS = 8
+CHUNKS = 16
 TILE = 256
+ORDERS = ((1, 0, 1), (1, 1, 0), (0, 0, 1), (0, 1, 0))
+LAG = 4
+AHEAD = 16
 VMEM_BYTES = 56 * 2**20
 
 
@@ -38,8 +41,12 @@
     total = 2**bits * rows
 
     def gather_order(c):
-        low = [0, 1] if c % 2 == 0 else [1, 0]
-        return list(range(2, bits)) + low
+        high = list(range(bits - 1, 1, -1))
+        choice = ORDERS[c % len(ORDERS)]
+        first, second = choice[1:]
+        if choice[0]:
+            return [first] + high + [second]
+        return high + [first, second]
 
     def reduce_order(c):
         return gather_order(c)[::-1]
@@ -103,9 +110,16 @@
             send_sem=rs_send.at[c, level], recv_sem=rs_recv.at[c, level],
             device_id=partner[b], device_id_type=MESH)
 
-    for c in range(chunks):
+    def wave(levels):
+        pairs = [(c, level) for c in range(chunks) for level in range(levels)]
+        return sorted(pairs, key=lambda p: (p[0] + LAG * p[1], -p[1]))
+
+    def begin(c):
         locals_[c].wait()
         ag_copy(c, 0).start()
+
+    for c in range(min(AHEAD, chunks)):
+        begin(c)
     locals_[chunks].wait()
     sc_copy(0).start()
     w_far = [pltpu.make_async_remote_copy(
@@ -114,16 +128,18 @@
     for copy in w_far:
         copy.start()
 
-    for level in range(bits):
-        for c in range(chunks):
-            ag_copy(c, level).wait_recv()
-            if level + 1 < bits:
-                ag_copy(c, level + 1).start()
-                continue
+    for c, level in wave(bits):
+        ag_copy(c, level).wait_recv()
+        if level == 0 and c + AHEAD < chunks:
+            begin(c + AHEAD)
+        if level + 1 < bits:
+            ag_copy(c, level + 1).start()
+        else:
             if c == 0:
                 for i in range(2):
                     w_own[i].wait()
                     w_far[i].wait_recv()
+
             def up_tile(j, _, c=c):
                 at = pl.ds(pl.multiple_of(j * TILE, TILE), TILE)
                 x = got[c].reshape(total, cols)
@@ -135,9 +151,10 @@
                 return 0
 
             lax.fori_loop(0, 2 * full // TILE, up_tile, 0)
-        sc_copy(level).wait_recv()
-        if level + 1 < bits:
-            sc_copy(level + 1).start()
+        if c == 0:
+            sc_copy(level).wait_recv()
+            if level + 1 < bits:
+                sc_copy(level + 1).start()
 
     def act_tile(j, _):
         at = pl.ds(pl.multiple_of(j * 128, 128), 128)
@@ -154,30 +171,30 @@
     w_own[2].wait()
     w_far[2].wait_recv()
 
-    for c in range(chunks):
-        def down_tile(j, _, c=c):
-            at = pl.ds(pl.multiple_of(c * cols + j * TILE, TILE), TILE)
-            y = jnp.dot(hidden[...], wd[:, at], preferred_element_type=jnp.float32)
-            y = (y * scale_col[:, :1]).astype(jnp.bfloat16)
-            to = (c, *([slice(None)] * (bits + 1)), pl.ds(pl.multiple_of(j * TILE, TILE), TILE))
-            part[to] = y.reshape((2,) * bits + (rows, TILE))
-            return 0
-
-        lax.fori_loop(0, cols // TILE, down_tile, 0)
-        rs_copy(c, 0).start()
-
-    for level in range(bits):
-        for c in range(chunks):
-            rs_copy(c, level).wait_recv()
-            order = reduce_order(c)
-            rest, b = order[level + 1:], order[level]
-            keep, came = (c, *place(rest)), (c, *place(rest, b))
-            value = part[keep].astype(jnp.float32) + landed[came].astype(jnp.float32)
-            if level + 1 < bits:
-                part[keep] = value.astype(jnp.bfloat16)
-                rs_copy(c, level + 1).start()
-            else:
-                out[:, pl.ds(c * cols, cols)] = value.astype(jnp.bfloat16)
+    for c, stage in wave(bits + 1):
+        if stage == 0:
+            def down_tile(j, _, c=c):
+                at = pl.ds(pl.multiple_of(c * cols + j * TILE, TILE), TILE)
+                y = jnp.dot(hidden[...], wd[:, at], preferred_element_type=jnp.float32)
+                y = (y * scale_col[:, :1]).astype(jnp.bfloat16)
+                to = (c, *([slice(None)] * (bits + 1)), pl.ds(pl.multiple_of(j * TILE, TILE), TILE))
+                part[to] = y.reshape((2,) * bits + (rows, TILE))
+                return 0
+
+            lax.fori_loop(0, cols // TILE, down_tile, 0)
+            rs_copy(c, 0).start()
+            continue
+        level = stage - 1
+        rs_copy(c, level).wait_recv()
+        order = reduce_order(c)
+        rest, b = order[level + 1:], order[level]
+        keep, came = (c, *place(rest)), (c, *place(rest, b))
+        value = part[keep].astype(jnp.float32) + landed[came].astype(jnp.float32)
+        if level + 1 < bits:
+            part[keep] = value.astype(jnp.bfloat16)
+            rs_copy(c, level + 1).start()
+        else:
+            out[:, pl.ds(c * cols, cols)] = value.astype(jnp.bfloat16)
 
     for level in range(bits):
         for c in range(chunks):

time: 118 us -> 103 us (0.87)
  Pallas kernels: 112 us -> 97.7 us
    pallas_call x1, Pallas kernels: 112 us -> 97.7 us  [fused(): pl.pallas_call(functools.partial(kernel, bits, CHUNKS), out_shape=jax.Sha...]
where the time goes in v2:
time: 103 us
  Pallas kernels  97.7 us (95%)
  other arithmetic  2.5 us (2%)
  local copies, waits for them, and re-layouts  2.28 us (2%)
    pallas_call x1, Pallas kernels, fused(): pl.pallas_call(functools.partial(kernel, bits, CHUNKS), out_shape=jax.Sha...  97.7 us

profile of v2, /device:TPU:0, one launch (start us, length us, event | category | flops | bytes accessed | tf_op | source)
XLA Modules:
  0.0 102.5 jit_solution(18038309973141174527)
XLA Ops:
  0.0 0.7 iota_compare_fusion.1
  0.7 0.9 fusion.2
  1.6 0.9 select_reduce_fusion
  2.5 0.6 pad.4.sc
  3.1 97.7 %shard_map.76 = bf16[32,4096]{1,0:T(8,128)(2,1)} custom-call(bf16[32,4096]{1,0:T(8,128)(2,1)} %bitcast.13, f32[32,128]{1,0:T(8,128)} %pad.4.sc, bf16[4096,384]{1,0:T(8,128)(2,1)} %bitcast.10, bf16[4096,384]{1,0:T(8,128)(2,1)} %bitcast.11, bf16[384,4096]{1,0:T(8,128)(2,1)} %bitcast.12), custom_call_target="tpu_custom_call" | custom-call | flops 9663676416 | bytes 18874368 | tf_op jit(solution)/shard_map/pallas_call | solution.py:232
  100.8 1.7 %copy.9 = bf16[4,8,4096]{2,1,0:T(8,128)(2,1)} copy(bf16[4,8,4096]{2,1,0:T(8,128)(2,1)} %bitcast.8) | data formatting | bytes 524288

commit v3 on v2

--- a/solution.py
+++ b/solution.py
@@ -20,8 +20,9 @@
 CHUNKS = 16
 TILE = 256
 ORDERS = ((1, 0, 1), (1, 1, 0), (0, 0, 1), (0, 1, 0))
-LAG = 4
-AHEAD = 16
+GATHER_LAG = 4
+REDUCE_LAG = 5
+AHEAD = 6
 VMEM_BYTES = 56 * 2**20
 
 
@@ -110,9 +111,9 @@
             send_sem=rs_send.at[c, level], recv_sem=rs_recv.at[c, level],
             device_id=partner[b], device_id_type=MESH)
 
-    def wave(levels):
+    def wave(levels, lag):
         pairs = [(c, level) for c in range(chunks) for level in range(levels)]
-        return sorted(pairs, key=lambda p: (p[0] + LAG * p[1], -p[1]))
+        return sorted(pairs, key=lambda p: (p[0] + lag * p[1], -p[1]))
 
     def begin(c):
         locals_[c].wait()
@@ -128,7 +129,7 @@
     for copy in w_far:
         copy.start()
 
-    for c, level in wave(bits):
+    for c, level in wave(bits, GATHER_LAG):
         ag_copy(c, level).wait_recv()
         if level == 0 and c + AHEAD < chunks:
             begin(c + AHEAD)
@@ -171,7 +172,7 @@
     w_own[2].wait()
     w_far[2].wait_recv()
 
-    for c, stage in wave(bits + 1):
+    for c, stage in wave(bits + 1, REDUCE_LAG):
         if stage == 0:
             def down_tile(j, _, c=c):
                 at = pl.ds(pl.multiple_of(c * cols + j * TILE, TILE), TILE)

time: 103 us -> 100 us (0.971)
  Pallas kernels: 97.7 us -> 95 us
    pallas_call x1, Pallas kernels: 97.7 us -> 95 us  [fused(): pl.pallas_call(functools.partial(kernel, bits, CHUNKS), out_shape=jax.Sha...]
where the time goes in v3:
time: 100 us; the launch traced here: 99.8 us
  Pallas kernels  95 us (95%)
  other arithmetic  2.5 us (2%)
  local copies, waits for them, and re-layouts  2.28 us (2%)
    pallas_call x1, Pallas kernels, fused(): pl.pallas_call(functools.partial(kernel, bits, CHUNKS), out_shape=jax.Sha...  95 us

profile of v3, /device:TPU:0, one launch (start us, length us, event | category | flops | bytes accessed | tf_op | source)
XLA Modules:
  0.0 99.8 jit_solution(4071128127112137484)
XLA Ops:
  0.0 0.7 iota_compare_fusion.1
  0.7 0.9 fusion.2
  1.6 0.9 select_reduce_fusion
  2.5 0.6 pad.4.sc
  3.1 95.0 %shard_map.76 = bf16[32,4096]{1,0:T(8,128)(2,1)} custom-call(bf16[32,4096]{1,0:T(8,128)(2,1)} %bitcast.13, f32[32,128]{1,0:T(8,128)} %pad.4.sc, bf16[4096,384]{1,0:T(8,128)(2,1)} %bitcast.10, bf16[4096,384]{1,0:T(8,128)(2,1)} %bitcast.11, bf16[384,4096]{1,0:T(8,128)(2,1)} %bitcast.12), custom_call_target="tpu_custom_call" | custom-call | flops 9663676416 | bytes 18874368 | tf_op jit(solution)/shard_map/pallas_call | solution.py:233
  98.2 1.7 %copy.9 = bf16[4,8,4096]{2,1,0:T(8,128)(2,1)} copy(bf16[4,8,4096]{2,1,0:T(8,128)(2,1)} %bitcast.8) | data formatting | bytes 524288

commit v4 on v3

--- a/solution.py
+++ b/solution.py
@@ -90,7 +90,8 @@
         order = gather_order(c)
         index = (c, *place(order[:level]))
         return pltpu.make_async_remote_copy(
-            src_ref=got.at[index], dst_ref=got.at[index],
+            src_ref=got.at[index] if level else tok.at[:, pl.ds(c * cols, cols)],
+            dst_ref=got.at[index],
             send_sem=ag_send.at[c, level], recv_sem=ag_recv.at[c, level],
             device_id=partner[order[level]], device_id_type=MESH)
 
@@ -116,7 +117,6 @@
         return sorted(pairs, key=lambda p: (p[0] + lag * p[1], -p[1]))
 
     def begin(c):
-        locals_[c].wait()
         ag_copy(c, 0).start()
 
     for c in range(min(AHEAD, chunks)):
@@ -131,6 +131,8 @@
 
     for c, level in wave(bits, GATHER_LAG):
         ag_copy(c, level).wait_recv()
+        if level == 0:
+            locals_[c].wait()
         if level == 0 and c + AHEAD < chunks:
             begin(c + AHEAD)
         if level + 1 < bits:

time: 100 us -> 100 us (level)
  no operation moved by 1% of the time
where the time goes in v4:
time: 100 us; the launch traced here: 99.5 us
  Pallas kernels  94.7 us (95%)
  other arithmetic  2.5 us (2%)
  local copies, waits for them, and re-layouts  2.28 us (2%)
    pallas_call x1, Pallas kernels, fused(): pl.pallas_call(functools.partial(kernel, bits, CHUNKS), out_shape=jax.Sha...  94.7 us

profile of v4, /device:TPU:0, one launch (start us, length us, event | category | flops | bytes accessed | tf_op | source)
XLA Modules:
  0.0 99.5 jit_solution(1006526906596035127)
XLA Ops:
  0.0 0.7 iota_compare_fusion.1
  0.7 0.9 fusion.2
  1.6 0.9 select_reduce_fusion
  2.5 0.6 pad.4.sc
  3.1 94.7 %shard_map.76 = bf16[32,4096]{1,0:T(8,128)(2,1)} custom-call(bf16[32,4096]{1,0:T(8,128)(2,1)} %bitcast.13, f32[32,128]{1,0:T(8,128)} %pad.4.sc, bf16[4096,384]{1,0:T(8,128)(2,1)} %bitcast.10, bf16[4096,384]{1,0:T(8,128)(2,1)} %bitcast.11, bf16[384,4096]{1,0:T(8,128)(2,1)} %bitcast.12), custom_call_target="tpu_custom_call" | custom-call | flops 9663676416 | bytes 18874368 | tf_op jit(solution)/shard_map/pallas_call | solution.py:235
  97.9 1.7 %copy.9 = bf16[4,8,4096]{2,1,0:T(8,128)(2,1)} copy(bf16[4,8,4096]{2,1,0:T(8,128)(2,1)} %bitcast.8) | data formatting | bytes 524288
